TPU v7x, 32 devices: a whole 2x2x4 slice. The times are simulated.
32 devices in a mesh: group: 2 (over x), expert: 4 (over y, core), dp: 4 (over z).
Axes of the slice: x: 2, y: 2, z: 4, core: 2. Of those that a mesh axis runs over, the one named last changes fastest.
Arguments:
- tokens: bfloat16 [1024, 7168], P(('group', 'expert', 'dp')), parts along dimension 0, may hold values from -6 to 6
- affinity: float32 [1024, 8], P(('group', 'expert', 'dp')), parts along dimension 0, may hold values from 0.05 to 1
- expert_ids: int32 [1024, 8], P(('group', 'expert', 'dp')), parts along dimension 0, may hold values from 0 to 255, as said below
- swap_partner: int32 [8], P('group'), parts along dimension 0, may hold values from 0 to 3, as said below
- gate_up: bfloat16 [4, 2, 7168, 1024], P('expert', None, None, 'dp'), may hold values from -6 to 6
- down_proj: bfloat16 [4, 1024, 7168], P('expert', 'dp'), may hold values from -6 to 6
Outputs:
- moe_out: bfloat16 [1024, 7168], P(('group', 'expert', 'dp')), parts along dimension 0
- new_gate_up: bfloat16 [8, 2, 7168, 1024], P(('group', 'expert'), None, None, 'dp'), parts along dimension 0
- new_down: bfloat16 [8, 1024, 7168], P(('group', 'expert'), 'dp'), parts along dimension 0
There are 2 independent parts, one for each index of `group`. A program takes and returns all parts, laid end to end along the dimension named above; an argument that names none is the same for every part. Nothing has to cross between parts.
Inputs may be any that keep to these rules, and one draw needn't show every extreme that they name: `expert_ids`: each row names 8 different experts. In each aligned block of 32 rows (the rows of one device), each expert below 4 is named by at most 2 rows, and one expert below 4 is named by exactly 2 rows in every block. swap_partner[e] is e or the slot 2 away from e (e + 4 / 2 modulo 4), swap_partner[swap_partner[e]] = e, and at least one pair of slots swaps.
All inputs are finite; a program needn't handle non-finite values.
Results may differ from a plain program's by a relative error of at most 0.009.
Values may be sent and summed in bfloat16 or wider, within the bound.
A program may use at most 64 MiB of HBM per device.

v0:
```python
import jax
import jax.numpy as jnp
from jax import lax
from jax.sharding import PartitionSpec as P

D = 7168
HID = 1024
CAP = 2


scale_mix = 2.5


def from_partner(shard, axis, distance):
    return lax.ppermute(shard, axis, [(i, i ^ 1 << distance) for i in range(lax.axis_size(axis))])


def expert_rows(row_block, gate_up_use, down_use):
    projected = jnp.einsum(
        "rd,gdh->grh", row_block, gate_up_use, preferred_element_type=jnp.float32
    ) * D ** (-0.5)
    hidden = (jax.nn.silu(projected[0]) * projected[1]).astype(jnp.bfloat16)
    partial_out = jnp.dot(hidden, down_use, preferred_element_type=jnp.float32) * HID ** (-0.5)
    return partial_out.astype(jnp.bfloat16)


def per_device(tokens, affinity, expert_ids, swap_partner, gate_up, down_proj):
    experts_here = lax.axis_size("expert")
    dp_size = lax.axis_size("dp")
    slot_count = experts_here * CAP
    model_width = tokens.shape[1]
    top_bit = experts_here.bit_length() - 2
    swapped_in = from_partner((gate_up, down_proj), "expert", top_bit)
    myself = lax.axis_index("expert")
    changed = swap_partner[myself] != myself
    new_gate_up = jnp.where(changed, swapped_in[0], gate_up)
    new_down = jnp.where(changed, swapped_in[1], down_proj)
    mixing = scale_mix * affinity / jnp.sum(affinity, axis=1, keepdims=True)
    inside = expert_ids < experts_here
    expert_range = jnp.arange(experts_here, dtype=jnp.int32)
    chosen = (expert_ids[:, :, None] == expert_range[None, None, :]).astype(jnp.int32)
    per_token = jnp.sum(chosen, axis=1)
    rank_table = jnp.cumsum(per_token, axis=0) - per_token
    pick_rank = jnp.sum(chosen * rank_table[:, None, :], axis=2)
    clipped = jnp.minimum(expert_ids, experts_here - 1)
    gate_up_use = gate_up[0]
    down_use = down_proj[0]
    position = clipped * CAP + pick_rank
    matches = (
        position[:, :, None] == jnp.arange(slot_count, dtype=jnp.int32)[None, None, :]
    ) & inside[:, :, None]
    dispatch = jnp.any(matches, axis=1).astype(jnp.bfloat16)
    combine = jnp.sum(jnp.where(matches, mixing[:, :, None], 0.0), axis=1)
    outgoing = lax.dot_general(
        dispatch, tokens, (((0,), (0,)), ((), ())), preferred_element_type=jnp.float32
    ).astype(jnp.bfloat16)
    fanned = jnp.broadcast_to(
        outgoing.reshape(experts_here, 1, CAP, model_width),
        (experts_here, dp_size, CAP, model_width),
    )
    fanned = fanned.reshape(experts_here * dp_size, CAP, model_width)
    arrived = lax.all_to_all(fanned, ("expert", "dp"), split_axis=0, concat_axis=0, tiled=True)
    flat_rows = arrived.reshape(-1, model_width)
    out_part = expert_rows(flat_rows, gate_up_use, down_use).reshape(arrived.shape)
    returned = lax.all_to_all(out_part, ("expert", "dp"), split_axis=0, concat_axis=0, tiled=True)
    summed = jnp.sum(
        returned.reshape(experts_here, dp_size, CAP, model_width), axis=1, dtype=jnp.float32
    )
    summed = summed.reshape(slot_count, model_width)
    moe_out = jnp.dot(
        combine, summed, precision=lax.Precision.HIGHEST, preferred_element_type=jnp.float32
    )
    return (moe_out.astype(jnp.bfloat16), new_gate_up, new_down)


def solution(mesh):
    placed = (
        P(("group", "expert", "dp"), None),
        P(("group", "expert", "dp"), None),
        P(("group", "expert", "dp"), None),
        P("group"),
        P("expert", None, None, "dp"),
        P("expert", "dp", None),
    )
    return jax.shard_map(
        per_device,
        mesh=mesh,
        in_specs=placed,
        out_specs=(
            P(("group", "expert", "dp"), None),
            P(("group", "expert"), None, None, "dp"),
            P(("group", "expert"), "dp", None),
        ),
        check_vma=False,
    )
```

profile of v0, /device:TPU:0, one launch (start us, length us, event | category | flops | bytes accessed | tf_op | source)
XLA Modules:
  0.0 285.5 jit_solution(3268757777833314884)
XLA Ops:
  0.6 3.0 %collective-permute-start = (bf16[1,2,7168,256]{3,2,1,0:T(8,128)(2,1)}, bf16[1,2,7168,256]{3,2,1,0:T(8,128)(2,1)}, u32[]{:S(2)}, u32[]{:S(2)}) collective-permute-start(bf16[1,2,7168,256]{3,2,1,0:T(8,128)(2,1)} %param.10), channel_id=1, source_target_pairs={{0,8},{4,12},{8,0},{12,4},{1,9},{5,13},{9,1},{13,5},{2,10},{6,14},... | collective-permute-start | bytes 22020104 | tf_op jit(solution)/shard_map/ppermute | solution.py:15
  3.7 0.1 collective-permute-start.1
  3.8 0.7 broadcast_compare_fusion
  4.5 0.7 convert_reduce_fusion.1
  5.2 0.1 copy.13
  5.2 0.1 reduce_window_sum.11
  5.3 0.1 copy.15
  5.4 0.7 select_reduce_fusion.1
  6.1 0.7 multiply_add_fusion
  6.8 0.2 convolution_convert_fusion.1
  7.0 0.2 broadcast_in_dim.30
  7.3 237.8 %all_to_all.10 = bf16[16,2,7168]{2,1,0:T(2,128)(2,1)S(1)} all-to-all(bf16[16,2,7168]{2,1,0:T(2,128)(2,1)S(1)} %bitcast.25), channel_id=1, replica_groups=mesh['group'=2,'expert'=4,'dp'=4] {'expert','dp'}, dimensions={0} | all-to-all | bytes 917504 | tf_op jit(solution)/shard_map/all_to_all | solution.py:62
  245.1 0.2 reshape.43
  245.3 4.6 %fusion.7 = f32[2,32,256]{2,1,0:T(8,128)S(1)} fusion(bf16[32,7168,1]{1,0,2:T(8,128)(2,1)S(1)} %reshape.43, bf16[1,2,7168,256]{3,2,1,0:T(8,128)(2,1)} %param.10), kind=kOutput, calls=%fused_computation.10 | convolution fusion | flops 234897408 | bytes 7864320 | tf_op jit(solution)/shard_map/rd,gdh->grh/dot_general | solution.py:19
  249.9 0.7 fusion
  250.7 1.0 reshape.40
  251.6 6.2 %all-to-all-start.1 = ((bf16[16,2,7168]{2,1,0:T(2,128)(2,1)}), bf16[16,2,7168]{2,1,0:T(2,128)(2,1)S(1)}, u32[]{:S(2)}, u32[]{:S(2)}) async-start(bf16[16,2,7168]{2,1,0:T(2,128)(2,1)} %reshape.40), calls=%async_computation.1 | async-start | bytes 917504 | tf_op jit(solution)/shard_map/all_to_all | solution.py:65
  257.8 0.6 dynamic_slice.3
  259.1 13.0 %all-to-all-done.1 = bf16[16,2,7168]{2,1,0:T(2,128)(2,1)S(1)} async-done(((bf16[16,2,7168]{2,1,0:T(2,128)(2,1)}), bf16[16,2,7168]{2,1,0:T(2,128)(2,1)S(1)}, u32[]{:S(2)}, u32[]{:S(2)}) %all-to-all-start.1) | async-done | bytes 458784 | tf_op jit(solution)/shard_map/all_to_all | solution.py:65
  272.1 0.4 convert_reduce_fusion
  272.5 0.2 reshape.41
  272.7 1.7 convolution_convert_fusion
  274.4 4.3 %broadcast_select_fusion.1 = bf16[1,256,7168]{2,1,0:T(8,128)(2,1)} fusion(bf16[1,256,7168]{2,1,0:T(8,128)(2,1)} %collective-permute-done.1, bf16[1,256,7168]{2,1,0:T(8,128)(2,1)} %param.11, pred[]{:T(512)S(6)} %ne.3), kind=kLoop, calls=%fused_computation.8 | loop fusion | flops 1835008 | bytes 11010049 | tf_op jit(solution)/shard_map/jit(_where)/select_n | solution.py:37
  278.6 6.9 %broadcast_select_fusion = bf16[1,2,7168,256]{3,2,1,0:T(8,128)(2,1)} fusion(bf16[1,2,7168,256]{3,2,1,0:T(8,128)(2,1)} %collective-permute-done, bf16[1,2,7168,256]{3,2,1,0:T(8,128)(2,1)} %param.10, pred[]{:T(512)S(6)} %ne.3), kind=kLoop, calls=%fused_computation.6 | loop fusion | flops 3670016 | bytes 22020096 | tf_op jit(solution)/shard_map/jit(_where)/select_n | solution.py:36
  (16 shorter events, 0.2 us)
Async XLA Ops:
  0.6 6.2 %copy-start = (bf16[32,7168]{1,0:T(8,128)(2,1)S(1)}, bf16[32,7168]{1,0:T(8,128)(2,1)}, u32[]{:S(2)}) copy-start(bf16[32,7168]{1,0:T(8,128)(2,1)} %param.6) | copy-start | bytes 1376260
  0.6 278.0 %collective-permute-start = (bf16[1,2,7168,256]{3,2,1,0:T(8,128)(2,1)}, bf16[1,2,7168,256]{3,2,1,0:T(8,128)(2,1)}, u32[]{:S(2)}, u32[]{:S(2)}) collective-permute-start(bf16[1,2,7168,256]{3,2,1,0:T(8,128)(2,1)} %param.10), channel_id=1, source_target_pairs={{0,8},{4,12},{8,0},{12,4},{1,9},{5,13},{9,1},{13,5},{2,10},{6,14},... | collective-permute-start | bytes 22020104 | tf_op jit(solution)/shard_map/ppermute | solution.py:15
  3.7 270.7 %collective-permute-start.1 = (bf16[1,256,7168]{2,1,0:T(8,128)(2,1)}, bf16[1,256,7168]{2,1,0:T(8,128)(2,1)}, u32[]{:S(2)}, u32[]{:S(2)}) collective-permute-start(bf16[1,256,7168]{2,1,0:T(8,128)(2,1)} %param.11), channel_id=1, source_target_pairs={{0,8},{4,12},{8,0},{12,4},{1,9},{5,13},{9,1},{13,5},{2,10},{6,14},... | collective-permute-start | bytes 11010056 | tf_op jit(solution)/shard_map/ppermute | solution.py:15
  245.3 4.6 %copy-start.1 = (bf16[1,256,7168]{2,1,0:T(8,128)(2,1)S(1)}, bf16[1,256,7168]{2,1,0:T(8,128)(2,1)}, u32[]{:S(2)}) copy-start(bf16[1,256,7168]{2,1,0:T(8,128)(2,1)} %param.11) | copy-start | bytes 11010052
  249.9 7.9 %copy-start.3 = (s32[4]{0:T(128)S(1)}, s32[4]{0:T(128)}, u32[]{:S(2)}) copy-start(s32[4]{0:T(128)} %param.9) | copy-start | bytes 52
  249.9 9.1 %copy-start.2 = (f32[32,8]{0,1:T(8,128)S(1)}, f32[32,8]{0,1:T(8,128)}, u32[]{:S(2)}) copy-start(f32[32,8]{0,1:T(8,128)} %param.7) | copy-start | bytes 3076
  251.6 20.4 %all-to-all-start.1 = ((bf16[16,2,7168]{2,1,0:T(2,128)(2,1)}), bf16[16,2,7168]{2,1,0:T(2,128)(2,1)S(1)}, u32[]{:S(2)}, u32[]{:S(2)}) async-start(bf16[16,2,7168]{2,1,0:T(2,128)(2,1)} %reshape.40), calls=%async_computation.1 | async-start | bytes 917504 | tf_op jit(solution)/shard_map/all_to_all | solution.py:65
where the time goes:
time: 286 us
  blocking collectives  238 us (83%)
  other arithmetic  14.5 us (5%)
  waiting for transfers between devices  13 us (5%)
  starting transfers between devices  9.27 us (3%)
  matrix products  7.15 us (2%)
    all_to_all x1, blocking collectives, per_device(): lax.all_to_all(fanned, ('expert', 'dp'), split_axis=0, concat_axis=0, til...  238 us
    all_to_all x1, waiting for transfers between devices, per_device(): lax.all_to_all(out_part, ('expert', 'dp'), split_axis=0, concat_axis=0, t...  13 us
    select_n x1, other arithmetic, per_device(): new_gate_up = jnp.where(changed, swapped_in[0], gate_up)  6.89 us
    all_to_all x1, starting transfers between devices, per_device(): lax.all_to_all(out_part, ('expert', 'dp'), split_axis=0, concat_axis=0, t...  6.15 us
  transfers between devices with their start and end apart: 3, of which 1 were waited for; matrix products, arithmetic and copies ran while one was open for 6% of the time, Pallas kernels for 0%

commit v1 on v0

v1 whole, which is shorter than its diff:
```python
import functools

import jax
import jax.numpy as jnp
from jax import lax
from jax.experimental import pallas as pl
from jax.experimental.pallas import tpu as pltpu
from jax.sharding import PartitionSpec as P

CAP = 2
TILE_ROWS = 16
SEGS = TILE_ROWS // CAP
WINDOW = 4
GU_PIECES = 16
scale_mix = 2.5
MESH = pl.DeviceIdType.MESH


def kernel(
    n_expert,
    n_dp,
    ids_ref,
    aff_ref,
    tok_ref,
    gu_ref,
    dn_ref,
    sgu_ref,
    sdn_ref,
    moe_ref,
    send_buf,
    arrived,
    out_buf,
    returned,
    acc,
    down_acc,
    sums,
    gu_vmem,
    dn_vmem,
    load_sem,
    tok_send,
    tok_recv,
    ret_send,
    ret_recv,
    y_send,
    y_recv,
    x_send,
    x_recv,
):
    g = lax.axis_index("group")
    e = lax.axis_index("expert")
    d = lax.axis_index("dp")
    peers = n_expert * n_dp
    me = e * n_dp + d
    half = n_expert // 2
    partner = lax.rem(e + half, n_expert)
    other = 1 - g
    tokens, width = tok_ref.shape
    top = ids_ref.shape[0]
    seg = width * CAP // TILE_ROWS
    hid = gu_ref.shape[3]

    loads = [
        pltpu.make_async_copy(gu_ref.at[0], gu_vmem, load_sem.at[0]),
        pltpu.make_async_copy(dn_ref.at[0], dn_vmem, load_sem.at[1]),
    ]
    for load in loads:
        load.start()

    barrier = pltpu.get_barrier_semaphore()

    def greet(i, carry):
        p = lax.rem(me + i, peers)
        pl.semaphore_signal(
            barrier, inc=1, device_id=(g, p // n_dp, lax.rem(p, n_dp)), device_id_type=MESH
        )
        return carry

    lax.fori_loop(1, peers, greet, 0)
    pl.semaphore_signal(barrier, inc=1, device_id=(other, e, d), device_id_type=MESH)

    table_rows = n_expert * TILE_ROWS
    row = lax.broadcasted_iota(jnp.int32, (table_rows, tokens), 0)
    expert_of = row // TILE_ROWS
    place_of = lax.rem(row // SEGS, CAP)
    ids = ids_ref[...]
    aff = aff_ref[...]
    mixing = scale_mix * aff / jnp.sum(aff, axis=0, keepdims=True)
    picked = jnp.zeros((table_rows, tokens), jnp.float32)
    mixed = jnp.zeros((table_rows, tokens), jnp.float32)
    for i in range(top):
        hit = ids[i : i + 1, :] == expert_of
        picked = picked + jnp.where(hit, 1.0, 0.0)
        mixed = mixed + jnp.where(hit, mixing[i : i + 1, :], 0.0)
    earlier = lax.broadcasted_iota(jnp.int32, (tokens, tokens), 0) < lax.broadcasted_iota(
        jnp.int32, (tokens, tokens), 1
    )
    rank = jnp.dot(
        picked.astype(jnp.bfloat16),
        jnp.where(earlier, 1.0, 0.0).astype(jnp.bfloat16),
        preferred_element_type=jnp.float32,
    )
    chosen = (picked > 0.5) & (rank.astype(jnp.int32) == place_of)
    dispatch = jnp.where(chosen, 1.0, 0.0).astype(jnp.bfloat16)
    combine = jnp.where(chosen, mixed, 0.0)
    piece_row = lax.rem(lax.broadcasted_iota(jnp.int32, (table_rows, seg), 0), SEGS)
    outgoing = jnp.zeros((table_rows, seg), jnp.float32)
    for s in range(SEGS):
        part = jnp.dot(
            dispatch, tok_ref[:, s * seg : (s + 1) * seg], preferred_element_type=jnp.float32
        )
        outgoing = jnp.where(piece_row == s, part, outgoing)
    send_buf[...] = outgoing.astype(jnp.bfloat16).reshape(send_buf.shape)
    arrived[me] = send_buf[e]

    pl.semaphore_wait(barrier, peers)

    def token_copy(p, slot_there):
        return pltpu.make_async_remote_copy(
            src_ref=send_buf.at[p // n_dp],
            dst_ref=arrived.at[slot_there],
            send_sem=tok_send.at[p],
            recv_sem=tok_recv.at[slot_there],
            device_id=(g, p // n_dp, lax.rem(p, n_dp)),
            device_id_type=MESH,
        )

    def return_copy(p, slot_there):
        return pltpu.make_async_remote_copy(
            src_ref=out_buf.at[p],
            dst_ref=returned.at[slot_there],
            send_sem=ret_send.at[p],
            recv_sem=ret_recv.at[slot_there],
            device_id=(g, p // n_dp, lax.rem(p, n_dp)),
            device_id_type=MESH,
        )

    def each_peer(act):
        def step(i, carry):
            act(lax.rem(me + i, peers))
            return carry

        lax.fori_loop(1, peers, step, 0)

    each_peer(lambda p: token_copy(p, me).start())

    gu_rows = width // GU_PIECES
    dn_half = hid // 2
    dn_pieces = dn_half // TILE_ROWS
    pieces = GU_PIECES + dn_pieces

    def place(own, swapped, k, which):
        if k < GU_PIECES:
            rows = pl.ds(k * gu_rows, gu_rows)
            return gu_ref.at[0, which, rows] if own else sgu_ref.at[0, which, rows]
        start = pl.multiple_of(which * dn_half + (k - GU_PIECES) * TILE_ROWS, TILE_ROWS)
        rows = pl.ds(start, TILE_ROWS)
        return dn_ref.at[0, rows] if own else sdn_ref.at[0, rows]

    def to_partner(k):
        return pltpu.make_async_remote_copy(
            src_ref=place(True, False, k, g),
            dst_ref=place(False, True, k, g),
            send_sem=y_send.at[k],
            recv_sem=y_recv.at[k],
            device_id=(g, partner, d),
            device_id_type=MESH,
        )

    def to_group(k, which):
        return pltpu.make_async_remote_copy(
            src_ref=place(False, True, k, which),
            dst_ref=place(False, True, k, which),
            send_sem=x_send.at[k],
            recv_sem=x_recv.at[k],
            device_id=(other, e, d),
            device_id_type=MESH,
        )

    for k in range(min(WINDOW, pieces)):
        to_partner(k).start()

    def forward(k):
        copy = to_partner(k)
        copy.wait_recv()
        to_group(k, g).start()
        copy.wait_send()
        if k + WINDOW < pieces:
            to_partner(k + WINDOW).start()

    for load in loads:
        load.wait()
    each_peer(lambda p: token_copy(p, p).wait_recv())

    block = min(256, peers * TILE_ROWS)
    groups = block // TILE_ROWS

    def expert_block(b, carry):
        start = pl.multiple_of(b * groups, groups)
        rows_in = arrived[pl.ds(start, groups)].reshape(block, seg)
        piece = lax.rem(lax.broadcasted_iota(jnp.int32, (block, hid), 0), SEGS)
        for half_of in range(2):
            total = jnp.zeros((block, hid), jnp.float32)
            for s in range(SEGS):
                part = jnp.dot(
                    rows_in,
                    gu_vmem[half_of, s * seg : (s + 1) * seg, :],
                    preferred_element_type=jnp.float32,
                )
                total = total + jnp.where(piece == s, part, 0.0)
            acc[half_of] = jnp.sum(total.reshape(block // SEGS, SEGS, hid), axis=1)
        gate = acc[0] * width ** (-0.5)
        up = acc[1] * width ** (-0.5)
        hidden = gate / (1.0 + jnp.exp(-gate)) * up
        spread = jnp.broadcast_to(hidden[:, None, :], (block // SEGS, SEGS, hid))
        spread = spread.reshape(block, hid).astype(jnp.bfloat16)
        out_piece = lax.rem(lax.broadcasted_iota(jnp.int32, (block, seg), 0), SEGS)
        for s in range(SEGS):
            part = jnp.dot(
                spread,
                dn_vmem[:, s * seg : (s + 1) * seg],
                preferred_element_type=jnp.float32,
            )
            down_acc[...] = part if s == 0 else jnp.where(out_piece == s, part, down_acc[...])
        scaled = down_acc[...] * (hid * n_dp) ** (-0.5)
        out_buf[pl.ds(start, groups)] = scaled.astype(jnp.bfloat16).reshape(groups, TILE_ROWS, seg)
        return carry

    lax.fori_loop(0, peers * TILE_ROWS // block, expert_block, 0)
    returned[me] = out_buf[me]
    each_peer(lambda p: return_copy(p, me).start())

    late = pieces // 2
    for k in range(late):
        forward(k)

    each_peer(lambda p: return_copy(p, p).wait_recv())
    for j in range(n_expert):
        total = returned[j * n_dp].astype(jnp.float32)
        for i in range(1, n_dp):
            total = total + returned[j * n_dp + i].astype(jnp.float32)
        sums[j * TILE_ROWS : (j + 1) * TILE_ROWS, :] = total
    weights = combine.T
    column = lax.rem(lax.broadcasted_iota(jnp.int32, (tokens, table_rows), 1), SEGS)
    for s in range(SEGS):
        moe = jnp.dot(
            jnp.where(column == s, weights, 0.0),
            sums[...],
            precision=lax.Precision.HIGHEST,
            preferred_element_type=jnp.float32,
        )
        moe_ref[:, s * seg : (s + 1) * seg] = moe.astype(jnp.bfloat16)

    for k in range(late, pieces):
        forward(k)

    each_peer(lambda p: token_copy(p, p).wait_send())
    each_peer(lambda p: return_copy(p, p).wait_send())
    for k in range(pieces):
        to_group(k, g).wait_send()
        to_group(k, other).wait_recv()


def exchange(n_expert, n_dp, expert_ids, affinity, tokens, gate_up, down_proj):
    rows, width = tokens.shape
    hid = gate_up.shape[3]
    peers = n_expert * n_dp
    seg = width * CAP // TILE_ROWS
    block = min(256, peers * TILE_ROWS)
    pieces = GU_PIECES + hid // 2 // TILE_ROWS
    vmem = pl.BlockSpec(memory_space=pltpu.VMEM)
    hbm = pl.BlockSpec(memory_space=pl.ANY)
    return pl.pallas_call(
        functools.partial(kernel, n_expert, n_dp),
        out_shape=(
            jax.ShapeDtypeStruct(gate_up.shape, jnp.bfloat16),
            jax.ShapeDtypeStruct(down_proj.shape, jnp.bfloat16),
            jax.ShapeDtypeStruct(tokens.shape, jnp.bfloat16),
        ),
        in_specs=[vmem, vmem, vmem, hbm, hbm],
        out_specs=(hbm, hbm, vmem),
        scratch_shapes=[
            pltpu.VMEM((n_expert, TILE_ROWS, seg), jnp.bfloat16),
            pltpu.VMEM((peers, TILE_ROWS, seg), jnp.bfloat16),
            pltpu.VMEM((peers, TILE_ROWS, seg), jnp.bfloat16),
            pltpu.VMEM((peers, TILE_ROWS, seg), jnp.bfloat16),
            pltpu.VMEM((2, block // SEGS, hid), jnp.float32),
            pltpu.VMEM((block, seg), jnp.float32),
            pltpu.VMEM((n_expert * TILE_ROWS, seg), jnp.float32),
            pltpu.VMEM(gate_up.shape[1:], jnp.bfloat16),
            pltpu.VMEM(down_proj.shape[1:], jnp.bfloat16),
            pltpu.SemaphoreType.DMA((2,)),
            pltpu.SemaphoreType.DMA((peers,)),
            pltpu.SemaphoreType.DMA((peers,)),
            pltpu.SemaphoreType.DMA((peers,)),
            pltpu.SemaphoreType.DMA((peers,)),
            pltpu.SemaphoreType.DMA((pieces,)),
            pltpu.SemaphoreType.DMA((pieces,)),
            pltpu.SemaphoreType.DMA((pieces,)),
            pltpu.SemaphoreType.DMA((pieces,)),
        ],
        compiler_params=pltpu.CompilerParams(
            collective_id=0, has_side_effects=True, vmem_limit_bytes=40 * 2**20
        ),
        cost_estimate=pl.CostEstimate(
            flops=2 * peers * TILE_ROWS * 3 * hid * width,
            bytes_accessed=8 * hid * width * 3,
            transcendentals=peers * CAP * hid,
        ),
    )(expert_ids.T, affinity.T, tokens, gate_up, down_proj)


def per_device(n_expert, n_dp, tokens, affinity, expert_ids, swap_partner, gate_up, down_proj):
    swapped_gate_up, swapped_down, moe_out = exchange(
        n_expert, n_dp, expert_ids, affinity, tokens, gate_up, down_proj
    )
    myself = lax.axis_index("expert")
    changed = swap_partner[myself] != myself
    new_gate_up = jnp.where(changed, swapped_gate_up, gate_up)
    new_down = jnp.where(changed, swapped_down, down_proj)
    return (moe_out, new_gate_up, new_down)


def solution(mesh):
    placed = (
        P(("group", "expert", "dp"), None),
        P(("group", "expert", "dp"), None),
        P(("group", "expert", "dp"), None),
        P("group"),
        P("expert", None, None, "dp"),
        P("expert", "dp", None),
    )
    return jax.shard_map(
        functools.partial(per_device, mesh.shape["expert"], mesh.shape["dp"]),
        mesh=mesh,
        in_specs=placed,
        out_specs=(
            P(("group", "expert", "dp"), None),
            P(("group", "expert"), None, None, "dp"),
            P(("group", "expert"), "dp", None),
        ),
        check_vma=False,
    )
```

time: 286 us -> 162 us (0.57)
  blocking collectives: 238 us -> 0 us
  Pallas kernels: 0 us -> 145 us
  waiting for transfers between devices: 13 us -> 0 us
  starting transfers between devices: 9.27 us -> 0 us
  matrix products: 7.15 us -> 0 us
  other arithmetic: 14.5 us -> 9.11 us
  local copies, waits for them, and re-layouts: 2.38 us -> 6.43 us
    all_to_all x1 -> x0, blocking collectives: 238 us -> none  [per_device(): lax.all_to_all(fanned, ('expert', 'dp'), split_axis=0, concat_axis=0, til...]
    pallas_call x0 -> x1, Pallas kernels: none -> 145 us  [exchange(): pl.pallas_call(functools.partial(kernel, n_expert, n_dp), out_shape=(jax....]
    all_to_all x1 -> x0, waiting for transfers between devices: 13 us -> none  [per_device(): lax.all_to_all(out_part, ('expert', 'dp'), split_axis=0, concat_axis=0, t...]
    dot_general x4 -> x0, matrix products: 7.15 us -> none  [the longest x1 4.58 us: expert_rows(): jnp.einsum('rd,gdh->grh', row_block, gate_up_use, preferred_element_type=...]
    all_to_all x1 -> x0, starting transfers between devices: 6.15 us -> none  [per_device(): lax.all_to_all(out_part, ('expert', 'dp'), split_axis=0, concat_axis=0, t...]
    unnamed x8 -> x9, local copies, waits for them, and re-layouts: 0.03 us -> 5.19 us
    ppermute x2 -> x0, starting transfers between devices: 3.11 us -> none  [from_partner(): lax.ppermute(shard, axis, [(i, i ^ 1 << distance) for i in range(lax.axis...]
  transfers between devices with their start and end apart: 3 -> 0, of which waited for: 1 -> 0; matrix products, arithmetic and copies ran while one was open for 6% -> 0% of each run, Pallas kernels for 0% -> 0%
where the time goes in v1:
time: 162 us
  Pallas kernels  145 us (90%)
  other arithmetic  9.11 us (6%)
  local copies, waits for them, and re-layouts  6.43 us (4%)
    pallas_call x1, Pallas kernels, exchange(): pl.pallas_call(functools.partial(kernel, n_expert, n_dp), out_shape=(jax....  145 us
    select_n x1, other arithmetic, per_device(): new_gate_up = jnp.where(changed, swapped_gate_up, gate_up)  6.89 us
    unnamed x9, local copies, waits for them, and re-layouts  5.19 us

profile of v1, /device:TPU:0, one launch (start us, length us, event | category | flops | bytes accessed | tf_op | source)
XLA Modules:
  0.0 161.6 jit_solution(12390659070521666333)
XLA Ops:
  0.6 1.2 dynamic_slice.3
  2.5 0.0 copy-start
  2.5 2.0 %copy-done = bf16[1,256,7168]{2,1,0:T(8,128)(2,1)S(1)} copy-done((bf16[1,256,7168]{2,1,0:T(8,128)(2,1)S(1)}, bf16[1,256,7168]{2,1,0:T(8,128)(2,1)}, u32[]{:S(2)}) %copy-start) | copy-done | bytes 3670040
  4.6 0.0 copy-start.1
  4.6 1.0 copy-done.1
  5.6 0.0 copy-start.2
  5.6 0.7 copy-done.2
  6.3 0.0 copy-start.3
  6.3 0.7 copy-done.3
  7.0 144.7 %shard_map.85 = (bf16[1,2,7168,256]{3,2,1,0:T(8,128)(2,1)}, bf16[1,256,7168]{2,1,0:T(8,128)(2,1)S(1)}, bf16[32,7168]{1,0:T(8,128)(2,1)S(1)}) custom-call(s32[8,32]{1,0:T(8,128)S(1)} %bitcast.3, f32[8,32]{1,0:T(8,128)S(1)} %bitcast.4, bf16[32,7168]{1,0:T(8,128)(2,1)S(1)} %copy-done.1, bf16[1,2,7168,256]{3,2,1,0:T(8,128)(2,1)} %gu_ref.1, ...), custom_call_target="tpu_custom_call" | custom-call | flops 2818572288 | bytes 44040192 | tf_op jit(solution)/shard_map/pallas_call | solution.py:272
  151.7 2.2 %broadcast_select_fusion.1 = bf16[1,256,7168]{2,1,0:T(8,128)(2,1)} fusion(bf16[1,256,7168]{2,1,0:T(8,128)(2,1)S(1)} %get-tuple-element.8, bf16[1,256,7168]{2,1,0:T(8,128)(2,1)S(1)} %copy-done, pred[]{:T(512)S(6)} %ne.3), kind=kLoop, calls=%fused_computation.1 | loop fusion | flops 1835008 | bytes 11010049 | tf_op jit(solution)/shard_map/jit(_where)/select_n | solution.py:319
  153.9 6.9 %broadcast_select_fusion = bf16[1,2,7168,256]{3,2,1,0:T(8,128)(2,1)} fusion(bf16[1,2,7168,256]{3,2,1,0:T(8,128)(2,1)} %get-tuple-element.7, bf16[1,2,7168,256]{3,2,1,0:T(8,128)(2,1)} %gu_ref.1, pred[]{:T(512)S(6)} %ne.3), kind=kLoop, calls=%fused_computation | loop fusion | flops 3670016 | bytes 22020096 | tf_op jit(solution)/shard_map/jit(_where)/select_n | solution.py:318
  160.8 0.8 copy.10
Async XLA Ops:
  2.5 2.0 %copy-start = (bf16[1,256,7168]{2,1,0:T(8,128)(2,1)S(1)}, bf16[1,256,7168]{2,1,0:T(8,128)(2,1)}, u32[]{:S(2)}) copy-start(bf16[1,256,7168]{2,1,0:T(8,128)(2,1)} %dn_ref.1) | copy-start | bytes 11010052
  4.6 1.0 copy-start.1
  5.6 0.7 copy-start.2
  6.3 0.7 copy-start.3

commit v2 on v1

--- a/solution.py
+++ b/solution.py
@@ -10,8 +10,9 @@
 CAP = 2
 TILE_ROWS = 16
 SEGS = TILE_ROWS // CAP
-WINDOW = 4
+WINDOW = 5
 GU_PIECES = 16
+LAG = 3
 scale_mix = 2.5
 MESH = pl.DeviceIdType.MESH
 
@@ -19,14 +20,19 @@
 def kernel(
     n_expert,
     n_dp,
-    ids_ref,
-    aff_ref,
-    tok_ref,
+    ids_hbm,
+    aff_hbm,
+    swap_hbm,
+    tok_hbm,
     gu_ref,
     dn_ref,
     sgu_ref,
     sdn_ref,
     moe_ref,
+    ids_ref,
+    aff_ref,
+    swap_ref,
+    tok_ref,
     send_buf,
     arrived,
     out_buf,
@@ -63,7 +69,13 @@
         pltpu.make_async_copy(gu_ref.at[0], gu_vmem, load_sem.at[0]),
         pltpu.make_async_copy(dn_ref.at[0], dn_vmem, load_sem.at[1]),
     ]
-    for load in loads:
+    small = [
+        pltpu.make_async_copy(ids_hbm, ids_ref, load_sem.at[2]),
+        pltpu.make_async_copy(aff_hbm, aff_ref, load_sem.at[3]),
+        pltpu.make_async_copy(swap_hbm, swap_ref, load_sem.at[4]),
+        pltpu.make_async_copy(tok_hbm, tok_ref, load_sem.at[5]),
+    ]
+    for load in small:
         load.start()
 
     barrier = pltpu.get_barrier_semaphore()
@@ -77,6 +89,76 @@
 
     lax.fori_loop(1, peers, greet, 0)
     pl.semaphore_signal(barrier, inc=1, device_id=(other, e, d), device_id_type=MESH)
+
+    pl.semaphore_wait(barrier, peers)
+
+    def token_copy(p, slot_there):
+        return pltpu.make_async_remote_copy(
+            src_ref=send_buf.at[p // n_dp],
+            dst_ref=arrived.at[slot_there],
+            send_sem=tok_send.at[p],
+            recv_sem=tok_recv.at[slot_there],
+            device_id=(g, p // n_dp, lax.rem(p, n_dp)),
+            device_id_type=MESH,
+        )
+
+    def return_copy(p, slot_there):
+        return pltpu.make_async_remote_copy(
+            src_ref=out_buf.at[p],
+            dst_ref=returned.at[slot_there],
+            send_sem=ret_send.at[p],
+            recv_sem=ret_recv.at[slot_there],
+            device_id=(g, p // n_dp, lax.rem(p, n_dp)),
+            device_id_type=MESH,
+        )
+
+    def each_peer(act):
+        def step(i, carry):
+            act(lax.rem(me + i, peers))
+            return carry
+
+        lax.fori_loop(1, peers, step, 0)
+
+    gu_rows = width // GU_PIECES
+    dn_half = hid // 2
+    dn_pieces = dn_half // TILE_ROWS
+    pieces = GU_PIECES + dn_pieces
+    early, late = pieces // 4, pieces * 2 // 3
+
+    def place(own, swapped, k, which):
+        if k < GU_PIECES:
+            rows = pl.ds(k * gu_rows, gu_rows)
+            return gu_ref.at[0, which, rows] if own else sgu_ref.at[0, which, rows]
+        start = pl.multiple_of(which * dn_half + (k - GU_PIECES) * TILE_ROWS, TILE_ROWS)
+        rows = pl.ds(start, TILE_ROWS)
+        return dn_ref.at[0, rows] if own else sdn_ref.at[0, rows]
+
+    def to_partner(k):
+        return pltpu.make_async_remote_copy(
+            src_ref=place(True, False, k, g),
+            dst_ref=place(False, True, k, g),
+            send_sem=y_send.at[k],
+            recv_sem=y_recv.at[k],
+            device_id=(g, partner, d),
+            device_id_type=MESH,
+        )
+
+    def to_group(k, which):
+        return pltpu.make_async_remote_copy(
+            src_ref=place(False, True, k, which),
+            dst_ref=place(False, True, k, which),
+            send_sem=x_send.at[k],
+            recv_sem=x_recv.at[k],
+            device_id=(other, e, d),
+            device_id_type=MESH,
+        )
+
+    for k in range(min(WINDOW, pieces)):
+        to_partner(k).start()
+    for load in loads:
+        load.start()
+    for load in small:
+        load.wait()
 
     table_rows = n_expert * TILE_ROWS
     row = lax.broadcasted_iota(jnp.int32, (table_rows, tokens), 0)
@@ -112,72 +194,8 @@
     send_buf[...] = outgoing.astype(jnp.bfloat16).reshape(send_buf.shape)
     arrived[me] = send_buf[e]
 
-    pl.semaphore_wait(barrier, peers)
-
-    def token_copy(p, slot_there):
-        return pltpu.make_async_remote_copy(
-            src_ref=send_buf.at[p // n_dp],
-            dst_ref=arrived.at[slot_there],
-            send_sem=tok_send.at[p],
-            recv_sem=tok_recv.at[slot_there],
-            device_id=(g, p // n_dp, lax.rem(p, n_dp)),
-            device_id_type=MESH,
-        )
-
-    def return_copy(p, slot_there):
-        return pltpu.make_async_remote_copy(
-            src_ref=out_buf.at[p],
-            dst_ref=returned.at[slot_there],
-            send_sem=ret_send.at[p],
-            recv_sem=ret_recv.at[slot_there],
-            device_id=(g, p // n_dp, lax.rem(p, n_dp)),
-            device_id_type=MESH,
-        )
-
-    def each_peer(act):
-        def step(i, carry):
-            act(lax.rem(me + i, peers))
-            return carry
-
-        lax.fori_loop(1, peers, step, 0)
-
     each_peer(lambda p: token_copy(p, me).start())
-
-    gu_rows = width // GU_PIECES
-    dn_half = hid // 2
-    dn_pieces = dn_half // TILE_ROWS
-    pieces = GU_PIECES + dn_pieces
-
-    def place(own, swapped, k, which):
-        if k < GU_PIECES:
-            rows = pl.ds(k * gu_rows, gu_rows)
-            return gu_ref.at[0, which, rows] if own else sgu_ref.at[0, which, rows]
-        start = pl.multiple_of(which * dn_half + (k - GU_PIECES) * TILE_ROWS, TILE_ROWS)
-        rows = pl.ds(start, TILE_ROWS)
-        return dn_ref.at[0, rows] if own else sdn_ref.at[0, rows]
-
-    def to_partner(k):
-        return pltpu.make_async_remote_copy(
-            src_ref=place(True, False, k, g),
-            dst_ref=place(False, True, k, g),
-            send_sem=y_send.at[k],
-            recv_sem=y_recv.at[k],
-            device_id=(g, partner, d),
-            device_id_type=MESH,
-        )
-
-    def to_group(k, which):
-        return pltpu.make_async_remote_copy(
-            src_ref=place(False, True, k, which),
-            dst_ref=place(False, True, k, which),
-            send_sem=x_send.at[k],
-            recv_sem=x_recv.at[k],
-            device_id=(other, e, d),
-            device_id_type=MESH,
-        )
-
-    for k in range(min(WINDOW, pieces)):
-        to_partner(k).start()
+    changed = swap_ref[e] != e
 
     def forward(k):
         copy = to_partner(k)
@@ -187,6 +205,29 @@
         if k + WINDOW < pieces:
             to_partner(k + WINDOW).start()
 
+    def choose(k, which):
+        shape = (gu_rows, hid) if k < GU_PIECES else (TILE_ROWS, width)
+        took = jnp.broadcast_to(jnp.where(changed, 1, 0), shape) == 1
+        if k < GU_PIECES:
+            rows = pl.ds(k * gu_rows, gu_rows)
+            new = sgu_ref[0, which, rows].astype(jnp.float32)
+            old = gu_vmem[which, rows].astype(jnp.float32)
+            sgu_ref[0, which, rows] = jnp.where(took, new, old).astype(jnp.bfloat16)
+        else:
+            start = which * dn_half + (k - GU_PIECES) * TILE_ROWS
+            rows = pl.ds(pl.multiple_of(start, TILE_ROWS), TILE_ROWS)
+            new = sdn_ref[0, rows].astype(jnp.float32)
+            old = dn_vmem[rows].astype(jnp.float32)
+            sdn_ref[0, rows] = jnp.where(took, new, old).astype(jnp.bfloat16)
+
+    def settle(k):
+        to_group(k, g).wait_send()
+        choose(k, g)
+        to_group(k, other).wait_recv()
+        choose(k, other)
+
+    for k in range(early):
+        forward(k)
     for load in loads:
         load.wait()
     each_peer(lambda p: token_copy(p, p).wait_recv())
@@ -229,9 +270,11 @@
     returned[me] = out_buf[me]
     each_peer(lambda p: return_copy(p, me).start())
 
-    late = pieces // 2
-    for k in range(late):
+    for k in range(early - LAG):
+        settle(k)
+    for k in range(early, late):
         forward(k)
+        settle(k - LAG)
 
     each_peer(lambda p: return_copy(p, p).wait_recv())
     for j in range(n_expert):
@@ -252,15 +295,15 @@
 
     for k in range(late, pieces):
         forward(k)
+        settle(k - LAG)
 
     each_peer(lambda p: token_copy(p, p).wait_send())
     each_peer(lambda p: return_copy(p, p).wait_send())
-    for k in range(pieces):
-        to_group(k, g).wait_send()
-        to_group(k, other).wait_recv()
-
-
-def exchange(n_expert, n_dp, expert_ids, affinity, tokens, gate_up, down_proj):
+    for k in range(pieces - LAG, pieces):
+        settle(k)
+
+
+def exchange(n_expert, n_dp, expert_ids, affinity, swap_partner, tokens, gate_up, down_proj):
     rows, width = tokens.shape
     hid = gate_up.shape[3]
     peers = n_expert * n_dp
@@ -268,17 +311,21 @@
     block = min(256, peers * TILE_ROWS)
     pieces = GU_PIECES + hid // 2 // TILE_ROWS
     vmem = pl.BlockSpec(memory_space=pltpu.VMEM)
-    hbm = pl.BlockSpec(memory_space=pl.ANY)
+    hbm = pl.BlockSpec(memory_space=pltpu.HBM)
     return pl.pallas_call(
         functools.partial(kernel, n_expert, n_dp),
         out_shape=(
-            jax.ShapeDtypeStruct(gate_up.shape, jnp.bfloat16),
-            jax.ShapeDtypeStruct(down_proj.shape, jnp.bfloat16),
-            jax.ShapeDtypeStruct(tokens.shape, jnp.bfloat16),
+            pltpu.VMEM(gate_up.shape, jnp.bfloat16),
+            pltpu.VMEM(down_proj.shape, jnp.bfloat16),
+            pltpu.VMEM(tokens.shape, jnp.bfloat16),
         ),
-        in_specs=[vmem, vmem, vmem, hbm, hbm],
-        out_specs=(hbm, hbm, vmem),
+        in_specs=[hbm] * 6,
+        out_specs=(vmem, vmem, vmem),
         scratch_shapes=[
+            pltpu.VMEM(expert_ids.shape[::-1], jnp.int32),
+            pltpu.VMEM(affinity.shape[::-1], jnp.float32),
+            pltpu.SMEM(swap_partner.shape, jnp.int32),
+            pltpu.VMEM(tokens.shape, jnp.bfloat16),
             pltpu.VMEM((n_expert, TILE_ROWS, seg), jnp.bfloat16),
             pltpu.VMEM((peers, TILE_ROWS, seg), jnp.bfloat16),
             pltpu.VMEM((peers, TILE_ROWS, seg), jnp.bfloat16),
@@ -288,7 +335,7 @@
             pltpu.VMEM((n_expert * TILE_ROWS, seg), jnp.float32),
             pltpu.VMEM(gate_up.shape[1:], jnp.bfloat16),
             pltpu.VMEM(down_proj.shape[1:], jnp.bfloat16),
-            pltpu.SemaphoreType.DMA((2,)),
+            pltpu.SemaphoreType.DMA((6,)),
             pltpu.SemaphoreType.DMA((peers,)),
             pltpu.SemaphoreType.DMA((peers,)),
             pltpu.SemaphoreType.DMA((peers,)),
@@ -299,24 +346,20 @@
             pltpu.SemaphoreType.DMA((pieces,)),
         ],
         compiler_params=pltpu.CompilerParams(
-            collective_id=0, has_side_effects=True, vmem_limit_bytes=40 * 2**20
+            collective_id=0, has_side_effects=True, vmem_limit_bytes=52 * 2**20
         ),
         cost_estimate=pl.CostEstimate(
             flops=2 * peers * TILE_ROWS * 3 * hid * width,
             bytes_accessed=8 * hid * width * 3,
             transcendentals=peers * CAP * hid,
         ),
-    )(expert_ids.T, affinity.T, tokens, gate_up, down_proj)
+    )(expert_ids.T, affinity.T, swap_partner, tokens, gate_up, down_proj)
 
 
 def per_device(n_expert, n_dp, tokens, affinity, expert_ids, swap_partner, gate_up, down_proj):
-    swapped_gate_up, swapped_down, moe_out = exchange(
-        n_expert, n_dp, expert_ids, affinity, tokens, gate_up, down_proj
-    )
-    myself = lax.axis_index("expert")
-    changed = swap_partner[myself] != myself
-    new_gate_up = jnp.where(changed, swapped_gate_up, gate_up)
-    new_down = jnp.where(changed, swapped_down, down_proj)
+    new_gate_up, new_down, moe_out = exchange(
+        n_expert, n_dp, expert_ids, affinity, swap_partner, tokens, gate_up, down_proj
+    )
     return (moe_out, new_gate_up, new_down)
 
 

time: 162 us -> 151 us (0.932)
  other arithmetic: 9.11 us -> 0 us
    select_n x2 -> x0, other arithmetic: 9.11 us -> none  [the longest x1 6.89 us: per_device(): new_gate_up = jnp.where(changed, swapped_gate_up, gate_up)]
    unnamed x9 -> x3, local copies, waits for them, and re-layouts: 5.19 us -> 5.65 us
where the time goes in v2:
time: 151 us; the launch traced here: 150 us
  Pallas kernels  144 us (95%)
  local copies, waits for them, and re-layouts  5.65 us (4%)
    pallas_call x1, Pallas kernels, exchange(): pl.pallas_call(functools.partial(kernel, n_expert, n_dp), out_shape=(pltp...  144 us
    unnamed x3, local copies, waits for them, and re-layouts  5.65 us

profile of v2, /device:TPU:0, one launch (start us, length us, event | category | flops | bytes accessed | tf_op | source)
XLA Modules:
  0.0 150.4 jit_solution(12532836022819368926)
XLA Ops:
  0.6 144.1 %shard_map.85 = (bf16[1,2,7168,256]{3,2,1,0:T(8,128)(2,1)S(1)}, bf16[1,256,7168]{2,1,0:T(8,128)(2,1)S(1)}, bf16[32,7168]{1,0:T(8,128)(2,1)S(1)}) custom-call(s32[8,32]{1,0:T(8,128)} %bitcast.2, f32[8,32]{1,0:T(8,128)} %bitcast.3, s32[4]{0:T(128)} %swap_hbm.1, bf16[32,7168]{1,0:T(8,128)(2,1)} %tok_hbm.1, bf16[1,2,7168,256]{3,2,1,0:T(8,128)(2,1)} %gu_ref.1, ...), custom_call_target="tpu_custom_call" | custom-call | flops 2818572288 | bytes 44040192 | tf_op jit(solution)/shard_map/pallas_call | solution.py:315
  144.8 0.8 copy.12
  145.6 1.8 %copy.14 = bf16[1,256,7168]{2,1,0:T(8,128)(2,1)} copy(bf16[1,256,7168]{2,1,0:T(8,128)(2,1)S(1)} %get-tuple-element.11) | data formatting | bytes 7340032
  147.4 3.0 %copy.13 = bf16[1,2,7168,256]{3,2,1,0:T(8,128)(2,1)} copy(bf16[1,2,7168,256]{3,2,1,0:T(8,128)(2,1)S(1)} %get-tuple-element.10) | data formatting | bytes 14680064

commit v3 on v2

--- a/solution.py
+++ b/solution.py
@@ -11,7 +11,7 @@
 TILE_ROWS = 16
 SEGS = TILE_ROWS // CAP
 WINDOW = 5
-GU_PIECES = 16
+GU_PIECES = 32
 LAG = 3
 scale_mix = 2.5
 MESH = pl.DeviceIdType.MESH
@@ -126,6 +126,7 @@
     early, late = pieces // 4, pieces * 2 // 3
 
     def place(own, swapped, k, which):
+        k = pieces - 1 - k
         if k < GU_PIECES:
             rows = pl.ds(k * gu_rows, gu_rows)
             return gu_ref.at[0, which, rows] if own else sgu_ref.at[0, which, rows]
@@ -206,6 +207,7 @@
             to_partner(k + WINDOW).start()
 
     def choose(k, which):
+        k = pieces - 1 - k
         shape = (gu_rows, hid) if k < GU_PIECES else (TILE_ROWS, width)
         took = jnp.broadcast_to(jnp.where(changed, 1, 0), shape) == 1
         if k < GU_PIECES:

time: 151 us -> 149 us (0.987)
    pallas_call x1, Pallas kernels: 144 us -> 143 us  [exchange(): pl.pallas_call(functools.partial(kernel, n_expert, n_dp), out_shape=(pltp...]
where the time goes in v3:
time: 149 us
  Pallas kernels  143 us (96%)
  local copies, waits for them, and re-layouts  5.65 us (4%)
    pallas_call x1, Pallas kernels, exchange(): pl.pallas_call(functools.partial(kernel, n_expert, n_dp), out_shape=(pltp...  143 us
    unnamed x3, local copies, waits for them, and re-layouts  5.65 us

profile of v3, /device:TPU:0, one launch (start us, length us, event | category | flops | bytes accessed | tf_op | source)
XLA Modules:
  0.0 148.8 jit_solution(16185743842000416327)
XLA Ops:
  0.6 142.5 %shard_map.85 = (bf16[1,2,7168,256]{3,2,1,0:T(8,128)(2,1)S(1)}, bf16[1,256,7168]{2,1,0:T(8,128)(2,1)S(1)}, bf16[32,7168]{1,0:T(8,128)(2,1)S(1)}) custom-call(s32[8,32]{1,0:T(8,128)} %bitcast.2, f32[8,32]{1,0:T(8,128)} %bitcast.3, s32[4]{0:T(128)} %swap_hbm.1, bf16[32,7168]{1,0:T(8,128)(2,1)} %tok_hbm.1, bf16[1,2,7168,256]{3,2,1,0:T(8,128)(2,1)} %gu_ref.1, ...), custom_call_target="tpu_custom_call" | custom-call | flops 2818572288 | bytes 44040192 | tf_op jit(solution)/shard_map/pallas_call | solution.py:317
  143.2 0.8 copy.12
  143.9 1.8 %copy.14 = bf16[1,256,7168]{2,1,0:T(8,128)(2,1)} copy(bf16[1,256,7168]{2,1,0:T(8,128)(2,1)S(1)} %get-tuple-element.11) | data formatting | bytes 7340032
  145.8 3.0 %copy.13 = bf16[1,2,7168,256]{3,2,1,0:T(8,128)(2,1)} copy(bf16[1,2,7168,256]{3,2,1,0:T(8,128)(2,1)S(1)} %get-tuple-element.10) | data formatting | bytes 14680064
